TPU v7x, 32 devices: a whole 2x2x4 slice. The times are simulated.
32 devices in a mesh: ta: 16 (over z, y, x), row: 2 (over core).
Axes of the slice: x: 2, y: 2, z: 4, core: 2. Of those that a mesh axis runs over, the one named last changes fastest.
Arguments:
- movie: bfloat16 [2, 128, 128, 512], P('row', 'ta'), may hold values from -384 to 384
- shifts: int32 [2, 128, 4, 2], P('row', 'ta'), may hold values from -8 to 8
- footprint: bfloat16 [2, 128, 8, 512], P('row', 'ta'), may hold values from 0.25 to 1
- support: int32 [2, 128, 8, 512], P('row', 'ta'), may hold values 0 or 1
- neuron_ids: int32 [2, 128, 8], P('row', 'ta'), may hold values from 0 to 255, as said below
- owner_order: int32 [256], replicated, may hold values from 0 to 255, each once
- start_traces: float32 [256, 128], P(('ta', 'row')), may hold values from 0 to 2
Outputs:
- tile_movie: bfloat16 [2, 128, 128, 512], P('row', 'ta')
- traces: float32 [256, 128], P(('ta', 'row'))
Inputs may be any that keep to these rules, and one draw needn't show every extreme that they name: `neuron_ids`: the neurons named by one tile's slots are distinct. Slot 0 of tile t of slab s names neuron s * 128 + t, and every slot of that tile names a neuron within 12 of it, counted modulo 256. `owner_order`: A permutation of all neurons.
All inputs are finite; a program needn't handle non-finite values. No bound on the sum of `support` on one device may be relied on, other than what follows from the above.
Results may differ from a plain program's by a relative error of at most 0.004.
Values may be sent and summed in bfloat16 or wider, within the bound.
A program may use at most 64 MiB of HBM per device.

v0:
```python
import jax
import jax.numpy as jnp
from jax import lax
from jax.sharding import PartitionSpec as P

TH = 16
TW = 32
MAXS = 8
ITERS = 2


def smoothing_table(length):
    places = jnp.arange(length, dtype=jnp.float32)
    spread = places[:, None] - places[None, :]
    kernel = jnp.exp(-spread * spread / 32.0)
    return (kernel / jnp.sum(kernel, axis=0, keepdims=True)).astype(jnp.bfloat16)


def local(movie, shifts, footprint, support, neuron_ids, owner_order, start_traces):
    frame_stack = movie[0]
    frame_moves = shifts[0]
    frame_count, height, breadth = frame_stack.shape
    patch_count = frame_moves.shape[1]
    patch_width = breadth // patch_count
    window_width = patch_width + 2 * MAXS
    padded_cols = jnp.pad(frame_stack, ((0, 0), (0, 0), (MAXS, MAXS)))
    windows = jnp.stack(
        [
            padded_cols[:, :, patch * patch_width : patch * patch_width + window_width]
            for patch in range(patch_count)
        ],
        axis=2,
    )
    window_index = jnp.arange(window_width, dtype=jnp.int32)
    target_index = (
        jnp.arange(patch_width, dtype=jnp.int32)[None, None, None, :]
        + MAXS
        + frame_moves[:, :, 1][:, :, None, None]
    )
    column_tables = (window_index[None, None, :, None] == target_index).astype(jnp.bfloat16)
    blocks = jnp.einsum(
        "fhpa,fpax->fhpx", windows, column_tables, preferred_element_type=jnp.float32
    ).astype(jnp.bfloat16)
    row_index = jnp.arange(height, dtype=jnp.int32)
    row_source = row_index[None, None, :, None] + frame_moves[:, :, 0][:, :, None, None]
    row_tables = (row_index[None, None, None, :] == row_source).astype(jnp.bfloat16)
    registered = jnp.einsum(
        "fpyh,fhpx->fypx", row_tables, blocks, preferred_element_type=jnp.float32
    )
    registered = registered.astype(jnp.bfloat16).reshape(frame_count, height, breadth)
    table_wide = smoothing_table(breadth)
    table_tall = smoothing_table(height)
    wide = jnp.einsum(
        "fhw,wv->fhv", registered, table_wide, preferred_element_type=jnp.float32
    ).astype(jnp.bfloat16)
    smooth = jnp.einsum("hy,fhv->fyv", table_tall, wide, preferred_element_type=jnp.float32)
    filtered = (registered.astype(jnp.float32) - smooth).astype(jnp.bfloat16)
    tile_rows = height // TH
    tile_cols = breadth // TW
    tiled = filtered.reshape(frame_count, tile_rows, TH, tile_cols, TW).transpose(1, 3, 0, 2, 4)
    tiled = tiled.reshape(tile_rows * tile_cols, frame_count, TH * TW)
    tile_movie = lax.all_to_all(tiled, "ta", split_axis=0, concat_axis=1, tiled=True)
    tile_count, frame_total, tile_pixels = tile_movie.shape
    footprints = footprint[0] * support[0].astype(jnp.bfloat16)
    slot_count = footprints.shape[1]
    slot_total = tile_count * slot_count
    gram = jnp.einsum("tip,tjp->tij", footprints, footprints, preferred_element_type=jnp.float32)
    projected = jnp.einsum(
        "tip,tfp->tif", footprints, tile_movie, preferred_element_type=jnp.float32
    )
    neuron_total = owner_order.shape[0]
    owner_slots = owner_order[neuron_ids[0]].reshape(slot_total)
    selector = (owner_slots[:, None] == jnp.arange(neuron_total, dtype=jnp.int32)[None, :]).astype(
        jnp.float32
    )
    spreader = selector.T
    traces_own = start_traces
    highest = lax.Precision.HIGHEST
    coupling_cols = jnp.einsum(
        "tij,tjk->tik",
        gram,
        selector.reshape(tile_count, slot_count, neuron_total),
        precision=highest,
    )
    joined = jnp.concatenate(
        [
            coupling_cols.reshape(slot_total, neuron_total),
            projected.reshape(slot_total, frame_total),
        ],
        axis=1,
    )
    owner_sums = lax.psum_scatter(
        jnp.dot(spreader, joined, precision=highest), ("ta", "row"), scatter_dimension=0, tiled=True
    )
    coupling_own = owner_sums[:, :neuron_total]
    drive_own = owner_sums[:, neuron_total:]
    bound_own = 1.0 + jnp.sum(coupling_own, axis=1)
    for iteration in range(ITERS):
        product = jnp.dot(
            coupling_own,
            lax.all_gather(traces_own, ("ta", "row"), axis=0, tiled=True),
            precision=highest,
        )
        gradient = product - drive_own
        traces_own = jnp.maximum(traces_own - gradient / bound_own[:, None], 0.0)
    return (tile_movie[None], traces_own)


def solution(mesh):
    return jax.shard_map(
        local,
        mesh=mesh,
        in_specs=(
            P("row", "ta", None, None),
            P("row", "ta", None, None),
            P("row", "ta", None, None),
            P("row", "ta", None, None),
            P("row", "ta", None),
            P(),
            P(("ta", "row"), None),
        ),
        out_specs=(P("row", "ta", None, None), P(("ta", "row"), None)),
        check_vma=False,
    )
```

profile of v0, /device:TPU:0, one launch (start us, length us, event | category | flops | bytes accessed | tf_op | source)
XLA Modules:
  0.0 241.8 jit_solution(7974238199823820715)
XLA Ops:
  7.2 0.0 copy-start
  7.2 0.3 fusion.31
  7.5 0.1 fusion.52
  7.6 0.0 copy-start.4
  7.6 1.7 copy.33
  9.3 0.1 fusion.41
  9.4 0.0 copy-done.4
  9.4 0.1 copy.32
  9.5 0.1 copy.37
  9.6 0.1 iota_add_fusion
  9.6 2.1 fusion.3
  11.7 1.4 fusion.1
  13.1 0.5 copy.40
  13.7 3.8 %reshape.86 = bf16[8,8,16,16,32]{4,3,2,1,0:T(8,128)(2,1)} reshape(bf16[8,128,512]{2,1,0:T(8,128)(2,1)S(1)} %copy.40) | data formatting | bytes 2097152 | tf_op jit(solution)/shard_map/reshape | solution.py:60
  17.4 5.3 %copy.41 = bf16[8,16,8,16,32]{4,3,2,1,0:T(8,128)(2,1)} copy(bf16[8,16,8,16,32]{4,1,3,0,2:T(8,128)(2,1)} %bitcast.69) | data formatting | bytes 2097152 | tf_op jit(solution)/shard_map/transpose | solution.py:60
  22.8 6.8 %reshape.87 = bf16[128,8,512]{2,1,0:T(8,128)(2,1)} reshape(bf16[8,16,8,16,32]{4,3,2,1,0:T(8,128)(2,1)} %copy.41) | data formatting | bytes 2097152 | tf_op jit(solution)/shard_map/reshape | solution.py:61
  29.6 0.0 copy-start.5
  29.6 8.4 %all-to-all-start = ((bf16[128,8,512]{2,1,0:T(8,128)(2,1)}), bf16[128,8,512]{2,1,0:T(8,128)(2,1)S(1)}, u32[]{:S(2)}, u32[]{:S(2)}) async-start(bf16[128,8,512]{2,1,0:T(8,128)(2,1)} %reshape.87), calls=%async_computation | async-start | bytes 2097152 | tf_op jit(solution)/shard_map/all_to_all | solution.py:62
  38.0 0.0 all-reduce.4.cloned.1.call-start
  38.1 0.0 copy-done.5
  38.1 0.1 reshape.92
  38.2 0.0 copy-done
  38.2 0.0 copy-start.1
  38.2 0.0 copy-start.2
  38.2 0.8 gather_fusion
  39.0 0.0 copy-start.3
  39.0 0.1 reshape.91
  39.1 0.0 copy-done.1
  39.1 0.0 copy-done.2
  39.1 0.1 fusion.50
  39.2 0.2 convolution_bitcast_fusion
  39.5 23.0 %all-to-all-done = bf16[128,8,512]{2,1,0:T(8,128)(2,1)S(1)} async-done(((bf16[128,8,512]{2,1,0:T(8,128)(2,1)}), bf16[128,8,512]{2,1,0:T(8,128)(2,1)S(1)}, u32[]{:S(2)}, u32[]{:S(2)}) %all-to-all-start) | async-done | bytes 1048608 | tf_op jit(solution)/shard_map/all_to_all | solution.py:62
  62.5 0.4 convolution_bitcast_fusion.1
  62.8 1.2 fusion.43
  64.0 0.0 all-reduce.4.cloned.1.call-update
  64.1 0.0 copy-done.3
  64.1 41.1 %all_gather.6 = f32[256,128]{1,0:T(8,128)S(1)} all-gather(f32[8,128]{1,0:T(8,128)S(1)} %copy-done.3), channel_id=1, replica_groups=mesh['ta'=16,'row'=2] {'ta','row'}, dimensions={0}, use_global_device_ids=true | all-gather | bytes 135168 | tf_op jit(solution)/shard_map/all_gather | solution.py:101
  105.2 1.1 copy.52
  106.2 85.6 %all-reduce.4.cloned.1.call-done = f32[256,384]{1,0:T(8,128)} async-done(((f32[256,384]{1,0:T(8,128)}), f32[256,384]{1,0:T(8,128)}) %all-reduce.4.cloned.1.call-update) | async-done | bytes 393232
  191.9 0.8 dynamic-slice_reduce_fusion
  192.7 0.9 fusion.27
  193.6 39.9 %all_gather.7 = f32[256,128]{1,0:T(8,128)S(1)} all-gather(f32[8,128]{1,0:T(8,128)S(1)} %fusion.27), channel_id=1, replica_groups=mesh['ta'=16,'row'=2] {'ta','row'}, dimensions={0}, use_global_device_ids=true | all-gather | bytes 135168 | tf_op jit(solution)/shard_map/all_gather | solution.py:101
  233.5 1.5 fusion.24
  (6 shorter events, 0.0 us)
Async XLA Ops:
  7.2 31.0 %copy-start = (s32[256]{0:T(256)S(1)}, s32[256]{0:T(256)}, u32[]{:S(2)}) copy-start(s32[256]{0:T(256)} %param.12) | copy-start | bytes 3076
  7.6 1.8 copy-start.4
  29.6 8.5 %copy-start.5 = (s32[1,8,8]{2,1,0:T(8,128)S(1)}, s32[1,8,8]{2,1,0:T(8,128)}, u32[]{:S(2)}) copy-start(s32[1,8,8]{2,1,0:T(8,128)} %param.11) | copy-start | bytes 772
  29.6 32.9 %all-to-all-start = ((bf16[128,8,512]{2,1,0:T(8,128)(2,1)}), bf16[128,8,512]{2,1,0:T(8,128)(2,1)S(1)}, u32[]{:S(2)}, u32[]{:S(2)}) async-start(bf16[128,8,512]{2,1,0:T(8,128)(2,1)} %reshape.87), calls=%async_computation | async-start | bytes 2097152 | tf_op jit(solution)/shard_map/all_to_all | solution.py:62
  38.0 153.9 %all-reduce.4.cloned.1.call-start = ((), (), s32[]{:S(2)}) async-start(), calls=%async_computation.1 | async-start | bytes 786432
  38.2 0.9 copy-start.1
  38.2 0.9 copy-start.2
  39.0 25.1 %copy-start.3 = (f32[8,128]{1,0:T(8,128)S(1)}, f32[8,128]{1,0:T(8,128)}, u32[]{:S(2)}) copy-start(f32[8,128]{1,0:T(8,128)} %param.13) | copy-start | bytes 12292
Sparse Core Ops, SparseCore 0:
  64.2 127.6 all-reduce.3
where the time goes:
time: 242 us
  waiting for transfers between devices  109 us (45%)
  blocking collectives  81 us (33%)
  local copies, waits for them, and re-layouts  20.4 us (8%)
  between operations  14.2 us (6%)
  starting transfers between devices  8.49 us (4%)
  matrix products  7.76 us (3%)
    unnamed x2, waiting for transfers between devices  85.7 us
    all_gather x2, blocking collectives, local(): lax.all_gather(traces_own, ('ta', 'row'), axis=0, tiled=True)  81 us
    all_to_all x1, waiting for transfers between devices, local(): lax.all_to_all(tiled, 'ta', split_axis=0, concat_axis=1, tiled=True)  23 us
    all_to_all x1, starting transfers between devices, local(): lax.all_to_all(tiled, 'ta', split_axis=0, concat_axis=1, tiled=True)  8.44 us
    reshape x1, local copies, waits for them, and re-layouts, local(): tiled = tiled.reshape(tile_rows * tile_cols, frame_count, TH * TW)  6.78 us
    transpose x1, local copies, waits for them, and re-layouts, local(): filtered.reshape(frame_count, tile_rows, TH, tile_cols, TW)  5.33 us
  transfers between devices with their start and end apart: 2, of which 2 were waited for; matrix products, arithmetic and copies ran while one was open for 1% of the time, Pallas kernels for 0%

commit v1 on v0

v1 whole, which is shorter than its diff:
```python
import functools

import jax
import jax.numpy as jnp
import numpy as np
from jax import lax
from jax.experimental import pallas as pl
from jax.experimental.pallas import tpu as pltpu
from jax.sharding import PartitionSpec as P

TH = 16
TW = 32
MAXS = 8
REACH = 12
ITERS = 2
LANES = 128
CHUNK = 2
MESH = pl.DeviceIdType.MESH
F32 = jnp.float32
BF16 = jnp.bfloat16


def smoothing_table(length):
    places = np.arange(length, dtype=np.float32)
    spread = places[:, None] - places[None, :]
    kernel = np.exp(-spread * spread / np.float32(32.0)).astype(np.float32)
    return kernel / np.sum(kernel, axis=0, keepdims=True)


def row_of(place, height):
    tall = height // TH
    group = LANES // TW
    inner = TH // group
    return place % tall * TH + place // tall % inner * group + place // (tall * inner)


def split(x):
    high = x.astype(BF16)
    return high, (x - high.astype(F32)).astype(BF16)


def mm(a, b, contract=(1, 0)):
    return lax.dot_general(
        a, b, (((contract[0],), (contract[1],)), ((), ())), preferred_element_type=F32
    )


def pick(onehot, x, contract=(1, 0)):
    high, low = split(x)
    return mm(onehot, high, contract) + mm(onehot, low, contract)


def mm3(a, b):
    ah, al = a
    bh, bl = split(b)
    return mm(ah, bh) + (mm(ah, bl) + mm(al, bh))


def filter_frame(frame, moves, wide_table, tall_table, stage, slot):
    height, breadth = frame.shape
    patches = len(moves)
    width = breadth // patches
    image = frame.astype(F32)
    lane = lax.broadcasted_iota(jnp.int32, (height, width), 1)
    place = lax.broadcasted_iota(jnp.int32, (height, height), 0)
    wanted = row_of(place, height)
    source = lax.broadcasted_iota(jnp.int32, (height, height), 1)
    strips = []
    for patch, (dy, dx) in enumerate(moves):
        blank = jnp.zeros((height, width), F32)
        here = image[:, patch * width : (patch + 1) * width]
        left = image[:, (patch - 1) * width : patch * width] if patch else blank
        right = image[:, (patch + 1) * width : (patch + 2) * width] if patch < patches - 1 else blank
        turn = lax.rem(width - dx, width)
        beside = jnp.where(lane < width // 2, right, left)
        at = lane + dx
        inside = (at >= 0) & (at < width)
        moved = jnp.where(inside, pltpu.roll(here, turn, 1), pltpu.roll(beside, turn, 1))
        chosen = (source == wanted + dy).astype(F32).astype(BF16)
        strips.append(mm(chosen, moved.astype(BF16)))
    registered = jnp.concatenate(strips, axis=1)
    wide = mm(registered.astype(BF16), wide_table).astype(BF16)
    smooth = mm(tall_table, wide)
    filtered = (registered - smooth).astype(BF16).astype(F32)
    group = LANES // TW
    part = height // group
    tall = height // TH
    stride = (breadth // TW) * CHUNK
    which = lax.broadcasted_iota(jnp.int32, (part, LANES), 1) // TW
    for q in range(breadth // LANES):
        cols = [filtered[b * part : (b + 1) * part, q * LANES : (q + 1) * LANES] for b in range(group)]
        for r in range(group):
            out = None
            for b in range(group):
                shift = (b - r) * TW % LANES
                turned = pltpu.roll(cols[b], shift, 1) if shift else cols[b]
                out = turned if out is None else jnp.where(which == b, turned, out)
            for a in range(TH // group):
                stage[a, pl.ds((q * group + r) * CHUNK + slot, tall, stride=stride), :] = out[a * tall : (a + 1) * tall]


def filter_kernel(moves, movie, wide_table, tall_table, out, stage):
    chunk = pl.program_id(0)
    for slot in range(CHUNK):
        frame = chunk * CHUNK + slot
        shifts = [(moves[frame, 2 * p], moves[frame, 2 * p + 1]) for p in range(moves.shape[1] // 2)]
        filter_frame(movie[slot], shifts, wide_table[...], tall_table[...], stage, slot)
    for a in range(stage.shape[0]):
        out[0, :, a * LANES : (a + 1) * LANES] = stage[a].astype(BF16)


def trace_kernel(
    sizes,
    send, prints, support, ids, order, start,
    tiles_out, traces_out,
    land, stage, full, bands, starts, drives, projected,
    a2a_send, a2a_recv, band_send, band_recv, start_send, start_recv, drive_send, drive_recv,
):
    n_ta, n_row = sizes
    n_dev = n_ta * n_row
    chunks, _, rows, pixels = send.shape
    tiles, frames, _ = tiles_out.shape
    window = drives.shape[1]
    neurons = order.shape[1]
    own = start.shape[0]
    slots = prints.shape[0] // tiles
    local_frames = chunks * CHUNK
    ta, row = lax.axis_index("ta"), lax.axis_index("row")
    home = row * n_ta + ta
    owner = ta * n_row + row

    def others(body):
        def step(k, carry):
            body(lax.rem(home + k, n_dev))
            return carry
        lax.fori_loop(1, n_dev, step, 0)

    def device(n):
        return (lax.rem(n, n_ta), n // n_ta)

    barrier = pltpu.get_barrier_semaphore()
    others(lambda n: pl.semaphore_signal(barrier, inc=1, device_id=device(n), device_id_type=MESH))

    masked = prints[...] * support[...].astype(F32).astype(BF16)
    total = tiles * slots
    gram = mm(masked, masked, (1, 1))
    tile_a = lax.broadcasted_iota(jnp.int32, (total, total), 0) // slots
    tile_b = lax.broadcasted_iota(jnp.int32, (total, total), 1) // slots
    gram = jnp.where(tile_a == tile_b, gram, 0.0)
    spot = lax.rem(ids[...] - (home * tiles - REACH) + 2 * neurons, neurons)
    selector = (lax.broadcasted_iota(jnp.int32, (window, total), 0) == spot).astype(F32).astype(BF16)
    left = pick(selector, gram)
    high, low = split(left)
    band = mm(high, selector, (1, 1)) + mm(low, selector, (1, 1))
    folds = window // 8
    bands[home] = jnp.concatenate(
        [band[8 * k : 8 * k + 8] for k in range(folds)]
        + ([jnp.zeros((8, LANES - folds * window), F32)] if folds * window < LANES else []),
        axis=1,
    )
    starts[owner] = start[...]

    pl.semaphore_wait(barrier, n_dev - 1)

    def post(c, step):
        def go(k, carry):
            dest = lax.rem(ta + k, n_ta)
            pltpu.make_async_remote_copy(
                src_ref=send.at[c, dest], dst_ref=land.at[c, ta],
                send_sem=a2a_send.at[c], recv_sem=a2a_recv.at[c],
                device_id=(dest, row), device_id_type=MESH,
            ).start()
            return carry
        lax.fori_loop(1, n_ta, go, 0)

    def spread(buffer, index, send_sem, recv_sem):
        others(lambda n: pltpu.make_async_remote_copy(
            src_ref=buffer.at[index], dst_ref=buffer.at[index],
            send_sem=send_sem, recv_sem=recv_sem,
            device_id=device(n), device_id_type=MESH,
        ).start())

    def drain(buffer, sem):
        part = buffer.at[pl.ds(0, n_dev - 1)]
        pltpu.make_async_copy(part, part, sem).wait()

    spread(bands, home, band_send, band_recv)
    spread(starts, owner, start_send, start_recv)
    for c in range(chunks):
        post(c, None)
        land[c, ta] = send[c, ta]

    drain(bands, band_recv)
    drain(starts, start_recv)
    spots = lax.broadcasted_iota(jnp.int32, (n_dev * window, neurons), 0)
    names = lax.broadcasted_iota(jnp.int32, (n_dev * window, neurons), 1)
    named = lax.rem(spots // window * tiles + lax.rem(spots, window) - REACH + neurons, neurons)
    places = (named == names).astype(F32).astype(BF16)
    expand_a = lax.broadcasted_iota(jnp.int32, (window, neurons), 0)
    expand_b = lax.broadcasted_iota(jnp.int32, (window, neurons), 1)
    everyone = bands[...]
    stacked = jnp.concatenate(
        [everyone[:, :, window * k : window * k + window] for k in range(folds)], axis=1
    ).reshape(n_dev * window, window)
    expand = ((expand_a - REACH + neurons) % neurons == expand_b).astype(F32).astype(BF16)
    wide = pick_right(stacked, expand).reshape(n_dev, window, neurons)
    wide = jnp.concatenate(
        [(pltpu.roll(wide[n], n * tiles % neurons, 1) if n * tiles % neurons else wide[n])[None] for n in range(n_dev)],
        axis=0,
    ).reshape(n_dev * window, neurons)
    coupling = pick(places, wide, (0, 0))
    bound = 1.0 + jnp.sum(coupling, axis=1, keepdims=True)
    inverse = 1.0 / bound
    owners = (lax.broadcasted_iota(jnp.int32, (neurons, neurons), 0) == order[...]).astype(F32).astype(BF16)
    mine = (
        lax.broadcasted_iota(jnp.int32, (own, neurons), 0) + owner * own == order[...]
    ).astype(F32).astype(BF16)
    current = pick(owners, starts[...].reshape(neurons, frames), (0, 0))
    parts = split(coupling)
    base = current - mm3(parts, current) * inverse

    for c in range(chunks):
        part = land.at[c, pl.ds(0, n_ta - 1)]
        pltpu.make_async_copy(part, part, a2a_recv.at[c]).wait()
        block = land[c].reshape(n_ta * rows, pixels)
        for a in range(pixels // LANES):
            stage[a] = block[:, a * LANES : (a + 1) * LANES].astype(F32)
        for tile in range(tiles):
            for f in range(CHUNK):
                full_rows = pl.ds(tile * frames + c * CHUNK + f, n_ta, stride=local_frames)
                from_rows = pl.ds(tile * CHUNK + f, n_ta, stride=tiles * CHUNK)
                for a in range(pixels // LANES):
                    full[a, full_rows, :] = stage[a, from_rows, :]
    for tile in range(tiles):
        block = jnp.concatenate(
            [full[a, tile * frames : (tile + 1) * frames] for a in range(pixels // LANES)], axis=1
        ).astype(BF16)
        tiles_out[tile] = block
        projected[tile * slots : (tile + 1) * slots] = mm(
            masked[tile * slots : (tile + 1) * slots], block, (1, 1)
        )
    drives[home] = pick(selector, projected[...]).astype(BF16)
    spread(drives, home, drive_send, drive_recv)
    drain(drives, drive_recv)
    drive = mm(places, drives[...].reshape(n_dev * window, frames), (0, 0))
    for iteration in range(ITERS):
        if iteration:
            base = current - mm3(parts, current) * inverse
        current = jnp.maximum(base + drive * inverse, 0.0)
    traces_out[...] = pick(mine, current)

    drain(bands, band_send)
    drain(starts, start_send)
    drain(drives, drive_send)
    for c in range(chunks):
        part = land.at[c, pl.ds(0, n_ta - 1)]
        pltpu.make_async_copy(part, part, a2a_send.at[c]).wait()


def pick_right(x, onehot):
    high, low = split(x)
    return mm(high, onehot) + mm(low, onehot)


def local(sizes, movie, shifts, footprint, support, neuron_ids, owner_order, start_traces):
    n_ta, n_row = sizes
    _, local_frames, height, breadth = movie.shape
    patches = shifts.shape[2]
    tile_total = (height // TH) * (breadth // TW)
    pixels = TH * TW
    tiles, slots = footprint.shape[1:3]
    neurons = owner_order.shape[0]
    own, frames = start_traces.shape
    chunks = local_frames // CHUNK
    order = np.asarray([row_of(k, height) for k in range(height)])
    tall = smoothing_table(height)[order][:, order].T
    vmem = pl.BlockSpec(memory_space=pltpu.VMEM)
    send = pl.pallas_call(
        filter_kernel,
        grid=(chunks,),
        out_shape=jax.ShapeDtypeStruct((chunks, tile_total * CHUNK, pixels), BF16),
        in_specs=[
            pl.BlockSpec(memory_space=pltpu.SMEM),
            pl.BlockSpec((CHUNK, height, breadth), lambda c: (c, 0, 0)),
            pl.BlockSpec((breadth, breadth), lambda c: (0, 0)),
            pl.BlockSpec((height, height), lambda c: (0, 0)),
        ],
        out_specs=pl.BlockSpec((1, tile_total * CHUNK, pixels), lambda c: (c, 0, 0)),
        scratch_shapes=[pltpu.VMEM((pixels // LANES, tile_total * CHUNK, LANES), F32)],
        compiler_params=pltpu.CompilerParams(vmem_limit_bytes=24 * 2**20),
        name="filter",
    )(
        shifts[0].reshape(local_frames, patches * 2),
        movie[0],
        jnp.asarray(smoothing_table(breadth).astype(jnp.bfloat16)),
        jnp.asarray(tall.astype(jnp.bfloat16)),
    )
    rows = tiles * CHUNK
    send = send.reshape(chunks, n_ta, rows, pixels)
    n_dev = n_ta * n_row
    window = -(-(tiles + 2 * REACH) // 8) * 8
    band_lanes = -(-(window // 8 * window) // LANES) * LANES
    dma = pltpu.SemaphoreType.DMA
    tile_movie, traces = pl.pallas_call(
        functools.partial(trace_kernel, sizes),
        out_shape=(
            jax.ShapeDtypeStruct((tiles, frames, pixels), BF16),
            jax.ShapeDtypeStruct((own, frames), F32),
        ),
        in_specs=[vmem] * 6,
        out_specs=(vmem, vmem),
        scratch_shapes=[
            pltpu.VMEM((chunks, n_ta, rows, pixels), BF16),
            pltpu.VMEM((pixels // LANES, n_ta * rows, LANES), F32),
            pltpu.VMEM((pixels // LANES, tiles * frames, LANES), F32),
            pltpu.VMEM((n_dev, 8, band_lanes), F32),
            pltpu.VMEM((n_dev, own, frames), F32),
            pltpu.VMEM((n_dev, window, frames), BF16),
            pltpu.VMEM((tiles * slots, frames), F32),
            dma((chunks,)), dma((chunks,)), dma, dma, dma, dma, dma, dma,
        ],
        compiler_params=pltpu.CompilerParams(
            collective_id=0, has_side_effects=True, vmem_limit_bytes=56 * 2**20
        ),
        name="traces",
    )(
        send,
        footprint.reshape(tiles * slots, pixels),
        support.reshape(tiles * slots, pixels),
        neuron_ids.reshape(1, tiles * slots),
        owner_order.reshape(1, neurons),
        start_traces,
    )
    return tile_movie[None], traces


def solution(mesh):
    sizes = (mesh.shape["ta"], mesh.shape["row"])
    return jax.shard_map(
        functools.partial(local, sizes),
        mesh=mesh,
        in_specs=(
            P("row", "ta", None, None),
            P("row", "ta", None, None),
            P("row", "ta", None, None),
            P("row", "ta", None, None),
            P("row", "ta", None),
            P(),
            P(("ta", "row"), None),
        ),
        out_specs=(P("row", "ta", None, None), P(("ta", "row"), None)),
        check_vma=False,
    )
```

time: 242 us -> 63.6 us (0.26)
  waiting for transfers between devices: 109 us -> 0 us
  blocking collectives: 81 us -> 0 us
  Pallas kernels: 0 us -> 54.4 us
  between operations: 14.2 us -> 0.68 us
  local copies, waits for them, and re-layouts: 20.4 us -> 8.18 us
  starting transfers between devices: 8.49 us -> 0 us
  matrix products: 7.76 us -> 0 us
    unnamed x2 -> x0, waiting for transfers between devices: 85.7 us -> none
    all_gather x2 -> x0, blocking collectives: 81 us -> none  [local(): lax.all_gather(traces_own, ('ta', 'row'), axis=0, tiled=True)]
    pallas_call x0 -> x2, Pallas kernels: none -> 54.4 us  [the longest x1 47.7 us: local(): pl.pallas_call(functools.partial(trace_kernel, sizes), out_shape=(jax.Sha...]
    all_to_all x1 -> x0, waiting for transfers between devices: 23 us -> none  [local(): lax.all_to_all(tiled, 'ta', split_axis=0, concat_axis=1, tiled=True)]
    reshape x2 -> x1, local copies, waits for them, and re-layouts: 10.6 us -> 0.59 us  [local(): neuron_ids.reshape(1, tiles * slots)]
    all_to_all x1 -> x0, starting transfers between devices: 8.44 us -> none  [local(): lax.all_to_all(tiled, 'ta', split_axis=0, concat_axis=1, tiled=True)]
    dot_general x8 -> x0, matrix products: 7.76 us -> none  [the longest x2 2.35 us: local(): jnp.dot(coupling_own, lax.all_gather(traces_own, ('ta', 'row'), axis=0, t...]
    unnamed x14 -> x16, local copies, waits for them, and re-layouts: 1.7 us -> 7.52 us
  transfers between devices with their start and end apart: 2 -> 0, of which waited for: 2 -> 0; matrix products, arithmetic and copies ran while one was open for 1% -> 0% of each run, Pallas kernels for 0% -> 0%
where the time goes in v1:
time: 63.6 us; the launch traced here: 63.2 us
  Pallas kernels  54.4 us (86%)
  local copies, waits for them, and re-layouts  8.18 us (13%)
  between operations  0.68 us (1%)
    pallas_call x1, Pallas kernels, local(): pl.pallas_call(functools.partial(trace_kernel, sizes), out_shape=(jax.Sha...  47.7 us
    unnamed x16, local copies, waits for them, and re-layouts  7.52 us
    pallas_call x1, Pallas kernels, local(): pl.pallas_call(filter_kernel, grid=(chunks,), out_shape=jax.ShapeDtypeStr...  6.68 us

profile of v1, /device:TPU:0, one launch (start us, length us, event | category | flops | bytes accessed | tf_op | source)
XLA Modules:
  0.0 63.2 jit_solution(8878971079089514616)
XLA Ops:
  0.6 0.0 copy-start.4
  0.6 0.0 copy-start.5
  0.6 0.7 %copy-done.4 = s32[1,8,8]{2,1,0:T(8,128)S(1)} copy-done((s32[1,8,8]{2,1,0:T(8,128)S(1)}, s32[1,8,8]{2,1,0:T(8,128)}, u32[]{:S(2)}) %copy-start.4) | copy-done | bytes 280
  1.3 0.6 reshape.22.ids
  1.9 0.0 copy-done.5
  1.9 0.1 copy.11.moves
  2.0 0.0 copy-start.1
  2.0 1.2 %copy-done.1 = bf16[1,8,128,512]{3,2,1,0:T(8,128)(2,1)S(1)} copy-done((bf16[1,8,128,512]{3,2,1,0:T(8,128)(2,1)S(1)}, bf16[1,8,128,512]{3,2,1,0:T(8,128)(2,1)}, u32[]{:S(2)}) %copy-start.1) | copy-done | bytes 1048600
  3.2 0.0 copy-start.2
  3.2 1.0 %copy-done.2 = bf16[512,512]{1,0:T(8,128)(2,1)S(1)} copy-done((bf16[512,512]{1,0:T(8,128)(2,1)S(1)}, bf16[512,512]{1,0:T(8,128)(2,1)}, u32[]{:S(2)}) %copy-start.2) | copy-done | bytes 524312
  4.2 0.0 copy-start.3
  4.3 0.8 %copy-done.3 = bf16[128,128]{1,0:T(8,128)(2,1)S(1)} copy-done((bf16[128,128]{1,0:T(8,128)(2,1)S(1)}, bf16[128,128]{1,0:T(8,128)(2,1)}, u32[]{:S(2)}) %copy-start.3) | copy-done | bytes 32792
  5.0 6.7 %filter.1 = bf16[4,256,512]{2,1,0:T(8,128)(2,1)S(1)} custom-call(s32[8,8]{1,0:T(8,128)S(1)} %copy.11.moves, bf16[8,128,512]{2,1,0:T(8,128)(2,1)S(1)} %bitcast.8, bf16[512,512]{1,0:T(8,128)(2,1)S(1)} %copy-done.2, bf16[128,128]{1,0:T(8,128)(2,1)S(1)} %copy-done.3), custom_call_target="tpu_custom_call" | custom-call | tf_op jit(solution)/shard_map/filter/pallas_call | solution.py:278
  11.7 0.0 copy-start
  11.7 1.0 %copy-done = bf16[4,256,512]{2,1,0:T(8,128)(2,1)} copy-done((bf16[4,256,512]{2,1,0:T(8,128)(2,1)}, bf16[4,256,512]{2,1,0:T(8,128)(2,1)S(1)}, u32[]{:S(2)}) %copy-start) | copy-done | bytes 1048600
  12.7 47.7 %traces.1 = (bf16[8,128,512]{2,1,0:T(8,128)(2,1)}, f32[8,128]{1,0:T(8,128)}) custom-call(bf16[4,16,16,512]{3,2,1,0:T(8,128)(2,1)} %bitcast.7, bf16[64,512]{1,0:T(8,128)(2,1)} %bitcast.11, s32[64,512]{1,0:T(8,128)} %bitcast.10, s32[1,64]{1,0:T(1,128)} %reshape.22.ids, s32[1,256]{1,0:T(1,128)} %bitcast.13, f32[8,128]{1,0:T(8,128)} %start.1), custom_call_target="tpu_custom_call" | custom-call | tf_op jit(solution)/shard_map/traces/pallas_call | solution.py:304
  60.4 0.0 copy-start.6
  60.4 2.3 %copy.14 = bf16[1,8,128,512]{3,2,1,0:T(8,128)(2,1)} copy(bf16[1,8,128,512]{3,2,1,0:T(8,128)(2,1)} %bitcast.9) | data formatting | bytes 2097152
  62.6 0.0 copy-done.6
  62.6 0.6 copy.15
Async XLA Ops:
  0.6 0.7 %copy-start.4 = (s32[1,8,8]{2,1,0:T(8,128)S(1)}, s32[1,8,8]{2,1,0:T(8,128)}, u32[]{:S(2)}) copy-start(s32[1,8,8]{2,1,0:T(8,128)} %param.13) | copy-start | bytes 772
  0.6 1.3 %copy-start.5 = (s32[1,8,4,2]{1,3,2,0:T(2,128)S(1)}, s32[1,8,4,2]{1,3,2,0:T(2,128)}, u32[]{:S(2)}) copy-start(s32[1,8,4,2]{1,3,2,0:T(2,128)} %param.10) | copy-start | bytes 772
  2.0 1.2 %copy-start.1 = (bf16[1,8,128,512]{3,2,1,0:T(8,128)(2,1)S(1)}, bf16[1,8,128,512]{3,2,1,0:T(8,128)(2,1)}, u32[]{:S(2)}) copy-start(bf16[1,8,128,512]{3,2,1,0:T(8,128)(2,1)} %param.9) | copy-start | bytes 3145732
  3.2 1.0 %copy-start.2 = (bf16[512,512]{1,0:T(8,128)(2,1)S(1)}, bf16[512,512]{1,0:T(8,128)(2,1)}, u32[]{:S(2)}) copy-start(bf16[512,512]{1,0:T(8,128)(2,1)} %constant.4.clone.wide_table) | copy-start | bytes 1572868
  4.2 0.8 %copy-start.3 = (bf16[128,128]{1,0:T(8,128)(2,1)S(1)}, bf16[128,128]{1,0:T(8,128)(2,1)}, u32[]{:S(2)}) copy-start(bf16[128,128]{1,0:T(8,128)(2,1)} %constant.5.clone.tall_table) | copy-start | bytes 98308
  11.7 1.0 %copy-start = (bf16[4,256,512]{2,1,0:T(8,128)(2,1)}, bf16[4,256,512]{2,1,0:T(8,128)(2,1)S(1)}, u32[]{:S(2)}) copy-start(bf16[4,256,512]{2,1,0:T(8,128)(2,1)S(1)} %filter.1) | copy-start | bytes 3145732
  60.4 2.3 %copy-start.6 = (f32[8,128]{1,0:T(8,128)S(1)}, f32[8,128]{1,0:T(8,128)}, u32[]{:S(2)}) copy-start(f32[8,128]{1,0:T(8,128)} %get-tuple-element.9) | copy-start | bytes 12292

commit v2 on v1

--- a/solution.py
+++ b/solution.py
@@ -99,22 +99,12 @@
                 stage[a, pl.ds((q * group + r) * CHUNK + slot, tall, stride=stride), :] = out[a * tall : (a + 1) * tall]
 
 
-def filter_kernel(moves, movie, wide_table, tall_table, out, stage):
-    chunk = pl.program_id(0)
-    for slot in range(CHUNK):
-        frame = chunk * CHUNK + slot
-        shifts = [(moves[frame, 2 * p], moves[frame, 2 * p + 1]) for p in range(moves.shape[1] // 2)]
-        filter_frame(movie[slot], shifts, wide_table[...], tall_table[...], stage, slot)
-    for a in range(stage.shape[0]):
-        out[0, :, a * LANES : (a + 1) * LANES] = stage[a].astype(BF16)
-
-
 def trace_kernel(
     sizes,
-    send, prints, support, ids, order, start,
+    moves, movie, wide_table, tall_table, prints, support, ids, order, start,
     tiles_out, traces_out,
-    land, stage, full, bands, starts, drives, projected,
-    a2a_send, a2a_recv, band_send, band_recv, start_send, start_recv, drive_send, drive_recv,
+    frames_in, send, land, stage, full, bands, starts, drives, projected,
+    movie_sem, a2a_send, a2a_recv, band_send, band_recv, start_send, start_recv, drive_send, drive_recv,
 ):
     n_ta, n_row = sizes
     n_dev = n_ta * n_row
@@ -138,6 +128,12 @@
     def device(n):
         return (lax.rem(n, n_ta), n // n_ta)
 
+    def fetch(c):
+        piece = pl.ds(c * CHUNK, CHUNK)
+        return pltpu.make_async_copy(movie.at[piece], frames_in.at[piece], movie_sem.at[c])
+
+    for c in range(chunks):
+        fetch(c).start()
     barrier = pltpu.get_barrier_semaphore()
     others(lambda n: pl.semaphore_signal(barrier, inc=1, device_id=device(n), device_id_type=MESH))
 
@@ -160,9 +156,7 @@
     )
     starts[owner] = start[...]
 
-    pl.semaphore_wait(barrier, n_dev - 1)
-
-    def post(c, step):
+    def post(c):
         def go(k, carry):
             dest = lax.rem(ta + k, n_ta)
             pltpu.make_async_remote_copy(
@@ -184,11 +178,29 @@
         part = buffer.at[pl.ds(0, n_dev - 1)]
         pltpu.make_async_copy(part, part, sem).wait()
 
-    spread(bands, home, band_send, band_recv)
-    spread(starts, owner, start_send, start_recv)
-    for c in range(chunks):
-        post(c, None)
+    def produce(c, carry):
+        fetch(c).wait()
+        for slot in range(CHUNK):
+            frame = c * CHUNK + slot
+            shifts = [(moves[frame, 2 * p], moves[frame, 2 * p + 1]) for p in range(moves.shape[1] // 2)]
+            filter_frame(frames_in[frame], shifts, wide_table[...], tall_table[...], stage, slot)
+        for a in range(pixels // LANES):
+            send[c, :, :, a * LANES : (a + 1) * LANES] = stage[a].astype(BF16).reshape(n_ta, rows, LANES)
+
+        @pl.when(c == 0)
+        def _():
+            pl.semaphore_wait(barrier, n_dev - 1)
+
+        post(c)
         land[c, ta] = send[c, ta]
+
+        @pl.when(c == 0)
+        def _():
+            spread(bands, home, band_send, band_recv)
+            spread(starts, owner, start_send, start_recv)
+        return carry
+
+    lax.fori_loop(0, chunks, produce, 0)
 
     drain(bands, band_recv)
     drain(starts, start_recv)
@@ -266,7 +278,6 @@
     n_ta, n_row = sizes
     _, local_frames, height, breadth = movie.shape
     patches = shifts.shape[2]
-    tile_total = (height // TH) * (breadth // TW)
     pixels = TH * TW
     tiles, slots = footprint.shape[1:3]
     neurons = owner_order.shape[0]
@@ -275,28 +286,7 @@
     order = np.asarray([row_of(k, height) for k in range(height)])
     tall = smoothing_table(height)[order][:, order].T
     vmem = pl.BlockSpec(memory_space=pltpu.VMEM)
-    send = pl.pallas_call(
-        filter_kernel,
-        grid=(chunks,),
-        out_shape=jax.ShapeDtypeStruct((chunks, tile_total * CHUNK, pixels), BF16),
-        in_specs=[
-            pl.BlockSpec(memory_space=pltpu.SMEM),
-            pl.BlockSpec((CHUNK, height, breadth), lambda c: (c, 0, 0)),
-            pl.BlockSpec((breadth, breadth), lambda c: (0, 0)),
-            pl.BlockSpec((height, height), lambda c: (0, 0)),
-        ],
-        out_specs=pl.BlockSpec((1, tile_total * CHUNK, pixels), lambda c: (c, 0, 0)),
-        scratch_shapes=[pltpu.VMEM((pixels // LANES, tile_total * CHUNK, LANES), F32)],
-        compiler_params=pltpu.CompilerParams(vmem_limit_bytes=24 * 2**20),
-        name="filter",
-    )(
-        shifts[0].reshape(local_frames, patches * 2),
-        movie[0],
-        jnp.asarray(smoothing_table(breadth).astype(jnp.bfloat16)),
-        jnp.asarray(tall.astype(jnp.bfloat16)),
-    )
     rows = tiles * CHUNK
-    send = send.reshape(chunks, n_ta, rows, pixels)
     n_dev = n_ta * n_row
     window = -(-(tiles + 2 * REACH) // 8) * 8
     band_lanes = -(-(window // 8 * window) // LANES) * LANES
@@ -307,9 +297,11 @@
             jax.ShapeDtypeStruct((tiles, frames, pixels), BF16),
             jax.ShapeDtypeStruct((own, frames), F32),
         ),
-        in_specs=[vmem] * 6,
+        in_specs=[pl.BlockSpec(memory_space=pltpu.SMEM), pl.BlockSpec(memory_space=pl.ANY)] + [vmem] * 7,
         out_specs=(vmem, vmem),
         scratch_shapes=[
+            pltpu.VMEM((local_frames, height, breadth), BF16),
+            pltpu.VMEM((chunks, n_ta, rows, pixels), BF16),
             pltpu.VMEM((chunks, n_ta, rows, pixels), BF16),
             pltpu.VMEM((pixels // LANES, n_ta * rows, LANES), F32),
             pltpu.VMEM((pixels // LANES, tiles * frames, LANES), F32),
@@ -317,14 +309,17 @@
             pltpu.VMEM((n_dev, own, frames), F32),
             pltpu.VMEM((n_dev, window, frames), BF16),
             pltpu.VMEM((tiles * slots, frames), F32),
-            dma((chunks,)), dma((chunks,)), dma, dma, dma, dma, dma, dma,
+            dma((chunks,)), dma((chunks,)), dma((chunks,)), dma, dma, dma, dma, dma, dma,
         ],
         compiler_params=pltpu.CompilerParams(
             collective_id=0, has_side_effects=True, vmem_limit_bytes=56 * 2**20
         ),
         name="traces",
     )(
-        send,
+        shifts[0].reshape(local_frames, patches * 2),
+        movie[0],
+        jnp.asarray(smoothing_table(breadth).astype(jnp.bfloat16)),
+        jnp.asarray(tall.astype(jnp.bfloat16)),
         footprint.reshape(tiles * slots, pixels),
         support.reshape(tiles * slots, pixels),
         neuron_ids.reshape(1, tiles * slots),

time: 63.6 us -> 53.3 us (0.84)
  Pallas kernels: 54.4 us -> 47.6 us
  local copies, waits for them, and re-layouts: 8.18 us -> 4.78 us
    pallas_call x1 -> x0, Pallas kernels: 6.68 us -> none  [local(): pl.pallas_call(filter_kernel, grid=(chunks,), out_shape=jax.ShapeDtypeStr...]
    unnamed x16 -> x8, local copies, waits for them, and re-layouts: 7.52 us -> 3.53 us
where the time goes in v2:
time: 53.3 us; the launch traced here: 53.1 us
  Pallas kernels  47.6 us (89%)
  local copies, waits for them, and re-layouts  4.78 us (9%)
  between operations  0.66 us (1%)
    pallas_call x1, Pallas kernels, local(): pl.pallas_call(functools.partial(trace_kernel, sizes), out_shape=(jax.Sha...  47.6 us
    unnamed x8, local copies, waits for them, and re-layouts  3.53 us

profile of v2, /device:TPU:0, one launch (start us, length us, event | category | flops | bytes accessed | tf_op | source)
XLA Modules:
  0.0 53.1 jit_solution(7865391222605021078)
XLA Ops:
  0.6 0.0 copy-start
  0.6 0.0 copy-start.1
  0.6 0.7 %copy-done = s32[1,8,8]{2,1,0:T(8,128)S(1)} copy-done((s32[1,8,8]{2,1,0:T(8,128)S(1)}, s32[1,8,8]{2,1,0:T(8,128)}, u32[]{:S(2)}) %copy-start) | copy-done | bytes 280
  1.3 0.6 %reshape.18.ids = s32[1,64]{1,0:T(1,128)} reshape(s32[1,8,8]{2,1,0:T(8,128)S(1)} %copy-done) | data formatting | bytes 512 | tf_op jit(solution)/shard_map/reshape | solution.py:325
  1.9 0.0 copy-done.1
  1.9 0.7 %copy.11.moves = s32[8,8]{1,0:T(8,128)} copy(s32[8,8]{0,1:T(8,128)S(1)} %bitcast.10) | data formatting | bytes 512 | tf_op jit(solution)/shard_map/reshape;squeeze | solution.py:319
  2.6 47.6 %traces.1 = (bf16[8,128,512]{2,1,0:T(8,128)(2,1)}, f32[8,128]{1,0:T(8,128)}) custom-call(s32[8,8]{1,0:T(8,128)} %copy.11.moves, bf16[8,128,512]{2,1,0:T(8,128)(2,1)} %bitcast.6, bf16[512,512]{1,0:T(8,128)(2,1)} %constant.4.clone.wide_table, bf16[128,128]{1,0:T(8,128)(2,1)} %constant.5.clone.tall_table, bf16[64,512]{1,0:T(8,128)(2,1)} %bitcast.9, ...), custom_call_target="tpu_custom_call" | custom-call | tf_op jit(solution)/shard_map/traces/pallas_call | solution.py:294
  50.2 0.0 copy-start.2
  50.2 2.3 %copy.14 = bf16[1,8,128,512]{3,2,1,0:T(8,128)(2,1)} copy(bf16[1,8,128,512]{3,2,1,0:T(8,128)(2,1)} %bitcast.7) | data formatting | bytes 2097152
  52.5 0.0 copy-done.2
  52.5 0.6 %copy.15 = f32[8,128]{1,0:T(8,128)} copy(f32[8,128]{1,0:T(8,128)S(1)} %copy-done.2) | data formatting | bytes 8192
Async XLA Ops:
  0.6 0.7 %copy-start = (s32[1,8,8]{2,1,0:T(8,128)S(1)}, s32[1,8,8]{2,1,0:T(8,128)}, u32[]{:S(2)}) copy-start(s32[1,8,8]{2,1,0:T(8,128)} %param.13) | copy-start | bytes 772
  0.6 1.3 %copy-start.1 = (s32[1,8,4,2]{1,3,2,0:T(2,128)S(1)}, s32[1,8,4,2]{1,3,2,0:T(2,128)}, u32[]{:S(2)}) copy-start(s32[1,8,4,2]{1,3,2,0:T(2,128)} %param.10) | copy-start | bytes 772
  50.2 2.3 %copy-start.2 = (f32[8,128]{1,0:T(8,128)S(1)}, f32[8,128]{1,0:T(8,128)}, u32[]{:S(2)}) copy-start(f32[8,128]{1,0:T(8,128)} %get-tuple-element.9) | copy-start | bytes 12292

commit v3 on v2

--- a/solution.py
+++ b/solution.py
@@ -103,14 +103,16 @@
     sizes,
     moves, movie, wide_table, tall_table, prints, support, ids, order, start,
     tiles_out, traces_out,
-    frames_in, send, land, stage, full, bands, starts, drives, projected,
-    movie_sem, a2a_send, a2a_recv, band_send, band_recv, start_send, start_recv, drive_send, drive_recv,
+    frames_in, send, land, stage, full, tiles_vmem, masked_ref, bands, starts, partial, inbox, drives, projected,
+    movie_sem, tiles_sem, a2a_send, a2a_recv, gather_sems, inbox_send, inbox_recv,
 ):
     n_ta, n_row = sizes
     n_dev = n_ta * n_row
     chunks, _, rows, pixels = send.shape
     tiles, frames, _ = tiles_out.shape
-    window = drives.shape[1]
+    reach = inbox.shape[0] // 2
+    window = -(-(tiles + 2 * REACH) // 8) * 8
+    folds = window // 8
     neurons = order.shape[1]
     own = start.shape[0]
     slots = prints.shape[0] // tiles
@@ -119,11 +121,21 @@
     home = row * n_ta + ta
     owner = ta * n_row + row
 
-    def others(body):
+    def partner(k):
+        if n_ta & (n_ta - 1):
+            return lax.rem(ta + k, n_ta)
+        return ta ^ (n_ta - k)
+
+    def along(body):
         def step(k, carry):
-            body(lax.rem(home + k, n_dev))
+            body(partner(k))
             return carry
-        lax.fori_loop(1, n_dev, step, 0)
+        lax.fori_loop(1, n_ta, step, 0)
+
+    def near(body):
+        for e in range(2 * reach + 1):
+            if e != reach:
+                body(e, lax.rem(home + e - reach + n_dev, n_dev))
 
     def device(n):
         return (lax.rem(n, n_ta), n // n_ta)
@@ -135,79 +147,109 @@
     for c in range(chunks):
         fetch(c).start()
     barrier = pltpu.get_barrier_semaphore()
-    others(lambda n: pl.semaphore_signal(barrier, inc=1, device_id=device(n), device_id_type=MESH))
-
-    masked = prints[...] * support[...].astype(F32).astype(BF16)
-    total = tiles * slots
-    gram = mm(masked, masked, (1, 1))
-    tile_a = lax.broadcasted_iota(jnp.int32, (total, total), 0) // slots
-    tile_b = lax.broadcasted_iota(jnp.int32, (total, total), 1) // slots
-    gram = jnp.where(tile_a == tile_b, gram, 0.0)
-    spot = lax.rem(ids[...] - (home * tiles - REACH) + 2 * neurons, neurons)
-    selector = (lax.broadcasted_iota(jnp.int32, (window, total), 0) == spot).astype(F32).astype(BF16)
-    left = pick(selector, gram)
-    high, low = split(left)
-    band = mm(high, selector, (1, 1)) + mm(low, selector, (1, 1))
-    folds = window // 8
-    bands[home] = jnp.concatenate(
-        [band[8 * k : 8 * k + 8] for k in range(folds)]
-        + ([jnp.zeros((8, LANES - folds * window), F32)] if folds * window < LANES else []),
-        axis=1,
-    )
-    starts[owner] = start[...]
+
+    def greet(target):
+        pl.semaphore_signal(barrier, inc=1, device_id=target, device_id_type=MESH)
+
+    along(lambda other: greet((other, row)))
+    for k in range(1, n_row):
+        greet((ta, lax.rem(row + k, n_row)))
+    near(lambda e, n: greet(device(n)))
+    greeted = n_ta - 1 + n_row - 1 + 2 * reach
+
+    def names(first, count):
+        flat = jnp.concatenate([ids[t : t + 1] for t in range(tiles)], axis=1)
+        spot = lax.rem(flat - first + 2 * neurons, neurons)
+        total = tiles * slots
+        return (lax.broadcasted_iota(jnp.int32, (count, total), 0) == spot).astype(F32).astype(BF16)
+
+    def measure_tiles():
+        masked = prints[...] * support[...].astype(F32).astype(BF16)
+        masked_ref[...] = masked
+        total = tiles * slots
+        gram = mm(masked, masked, (1, 1))
+        tile_a = lax.broadcasted_iota(jnp.int32, (total, total), 0) // slots
+        tile_b = lax.broadcasted_iota(jnp.int32, (total, total), 1) // slots
+        gram = jnp.where(tile_a == tile_b, gram, 0.0)
+        selector = names(home * tiles - REACH, window)
+        high, low = split(pick(selector, gram))
+        band = mm(high, selector, (1, 1)) + mm(low, selector, (1, 1))
+        bands[home] = jnp.concatenate(
+            [band[8 * k : 8 * k + 8] for k in range(folds)]
+            + ([jnp.zeros((8, LANES - folds * window), F32)] if folds * window < LANES else []),
+            axis=1,
+        )
+        starts[home] = start[...]
 
     def post(c):
-        def go(k, carry):
-            dest = lax.rem(ta + k, n_ta)
+        along(lambda dest: pltpu.make_async_remote_copy(
+            src_ref=send.at[c, dest], dst_ref=land.at[c, ta],
+            send_sem=a2a_send.at[c], recv_sem=a2a_recv.at[c],
+            device_id=(dest, row), device_id_type=MESH,
+        ).start())
+
+    def wait(part, sem):
+        pltpu.make_async_copy(part, part, sem).wait()
+
+    def gather(buffer, which):
+        along(lambda other: pltpu.make_async_remote_copy(
+            src_ref=buffer.at[home], dst_ref=buffer.at[home],
+            send_sem=gather_sems.at[which, 0], recv_sem=gather_sems.at[which, 1],
+            device_id=(other, row), device_id_type=MESH,
+        ).start())
+
+    def relay(buffer, which):
+        wait(buffer.at[pl.ds(0, n_ta - 1)], gather_sems.at[which, 1])
+        slab = buffer.at[pl.ds(row * n_ta, n_ta)]
+        for k in range(1, n_row):
             pltpu.make_async_remote_copy(
-                src_ref=send.at[c, dest], dst_ref=land.at[c, ta],
-                send_sem=a2a_send.at[c], recv_sem=a2a_recv.at[c],
-                device_id=(dest, row), device_id_type=MESH,
+                src_ref=slab, dst_ref=slab,
+                send_sem=gather_sems.at[which, 2], recv_sem=gather_sems.at[which, 3],
+                device_id=(ta, lax.rem(row + k, n_row)), device_id_type=MESH,
             ).start()
-            return carry
-        lax.fori_loop(1, n_ta, go, 0)
-
-    def spread(buffer, index, send_sem, recv_sem):
-        others(lambda n: pltpu.make_async_remote_copy(
-            src_ref=buffer.at[index], dst_ref=buffer.at[index],
-            send_sem=send_sem, recv_sem=recv_sem,
-            device_id=device(n), device_id_type=MESH,
-        ).start())
-
-    def drain(buffer, sem):
-        part = buffer.at[pl.ds(0, n_dev - 1)]
-        pltpu.make_async_copy(part, part, sem).wait()
+
+    def gathered(buffer, which):
+        if n_row > 1:
+            wait(buffer.at[pl.ds(0, n_ta * (n_row - 1))], gather_sems.at[which, 3])
+
+    def sent(buffer, which):
+        wait(buffer.at[pl.ds(0, n_ta - 1)], gather_sems.at[which, 0])
+        if n_row > 1:
+            wait(buffer.at[pl.ds(0, n_ta * (n_row - 1))], gather_sems.at[which, 2])
 
     def produce(c, carry):
         fetch(c).wait()
         for slot in range(CHUNK):
             frame = c * CHUNK + slot
-            shifts = [(moves[frame, 2 * p], moves[frame, 2 * p + 1]) for p in range(moves.shape[1] // 2)]
+            shifts = [(moves[p, 0, frame], moves[p, 1, frame]) for p in range(moves.shape[0])]
             filter_frame(frames_in[frame], shifts, wide_table[...], tall_table[...], stage, slot)
         for a in range(pixels // LANES):
             send[c, :, :, a * LANES : (a + 1) * LANES] = stage[a].astype(BF16).reshape(n_ta, rows, LANES)
 
         @pl.when(c == 0)
         def _():
-            pl.semaphore_wait(barrier, n_dev - 1)
+            pl.semaphore_wait(barrier, greeted)
 
         post(c)
         land[c, ta] = send[c, ta]
 
         @pl.when(c == 0)
         def _():
-            spread(bands, home, band_send, band_recv)
-            spread(starts, owner, start_send, start_recv)
+            measure_tiles()
+            gather(bands, 0)
+            gather(starts, 1)
         return carry
 
     lax.fori_loop(0, chunks, produce, 0)
 
-    drain(bands, band_recv)
-    drain(starts, start_recv)
+    relay(bands, 0)
+    relay(starts, 1)
+    gathered(bands, 0)
+    gathered(starts, 1)
     spots = lax.broadcasted_iota(jnp.int32, (n_dev * window, neurons), 0)
-    names = lax.broadcasted_iota(jnp.int32, (n_dev * window, neurons), 1)
+    wanted = lax.broadcasted_iota(jnp.int32, (n_dev * window, neurons), 1)
     named = lax.rem(spots // window * tiles + lax.rem(spots, window) - REACH + neurons, neurons)
-    places = (named == names).astype(F32).astype(BF16)
+    places = (named == wanted).astype(F32).astype(BF16)
     expand_a = lax.broadcasted_iota(jnp.int32, (window, neurons), 0)
     expand_b = lax.broadcasted_iota(jnp.int32, (window, neurons), 1)
     everyone = bands[...]
@@ -223,7 +265,9 @@
     coupling = pick(places, wide, (0, 0))
     bound = 1.0 + jnp.sum(coupling, axis=1, keepdims=True)
     inverse = 1.0 / bound
-    owners = (lax.broadcasted_iota(jnp.int32, (neurons, neurons), 0) == order[...]).astype(F32).astype(BF16)
+    keeper = order[...] // own
+    spot = (keeper % n_row * n_ta + keeper // n_row) * own + order[...] % own
+    owners = (lax.broadcasted_iota(jnp.int32, (neurons, neurons), 0) == spot).astype(F32).astype(BF16)
     mine = (
         lax.broadcasted_iota(jnp.int32, (own, neurons), 0) + owner * own == order[...]
     ).astype(F32).astype(BF16)
@@ -232,8 +276,7 @@
     base = current - mm3(parts, current) * inverse
 
     for c in range(chunks):
-        part = land.at[c, pl.ds(0, n_ta - 1)]
-        pltpu.make_async_copy(part, part, a2a_recv.at[c]).wait()
+        wait(land.at[c, pl.ds(0, n_ta - 1)], a2a_recv.at[c])
         block = land[c].reshape(n_ta * rows, pixels)
         for a in range(pixels // LANES):
             stage[a] = block[:, a * LANES : (a + 1) * LANES].astype(F32)
@@ -247,26 +290,42 @@
         block = jnp.concatenate(
             [full[a, tile * frames : (tile + 1) * frames] for a in range(pixels // LANES)], axis=1
         ).astype(BF16)
-        tiles_out[tile] = block
+        tiles_vmem[tile] = block
         projected[tile * slots : (tile + 1) * slots] = mm(
-            masked[tile * slots : (tile + 1) * slots], block, (1, 1)
+            masked_ref[tile * slots : (tile + 1) * slots], block, (1, 1)
         )
-    drives[home] = pick(selector, projected[...]).astype(BF16)
-    spread(drives, home, drive_send, drive_recv)
-    drain(drives, drive_recv)
-    drive = mm(places, drives[...].reshape(n_dev * window, frames), (0, 0))
+    whole = pltpu.make_async_copy(tiles_vmem, tiles_out, tiles_sem)
+    terms = pick(names((home - reach) * tiles, (2 * reach + 1) * tiles), projected[...])
+    partial[...] = terms.reshape(2 * reach + 1, tiles, frames)
+
+    near(lambda e, n: pltpu.make_async_remote_copy(
+        src_ref=partial.at[e], dst_ref=inbox.at[e],
+        send_sem=inbox_send, recv_sem=inbox_recv,
+        device_id=device(n), device_id_type=MESH,
+    ).start())
+    whole.start()
+    wait(inbox.at[pl.ds(0, 2 * reach)], inbox_recv)
+    mine_drive = partial[reach]
+    for e in range(2 * reach + 1):
+        if e != reach:
+            mine_drive = mine_drive + inbox[e]
+    drives[home] = mine_drive
+    gather(drives, 2)
+    relay(drives, 2)
+    gathered(drives, 2)
+    drive = drives[...].reshape(neurons, frames)
     for iteration in range(ITERS):
         if iteration:
             base = current - mm3(parts, current) * inverse
         current = jnp.maximum(base + drive * inverse, 0.0)
     traces_out[...] = pick(mine, current)
 
-    drain(bands, band_send)
-    drain(starts, start_send)
-    drain(drives, drive_send)
+    for which, buffer in enumerate((bands, starts, drives)):
+        sent(buffer, which)
+    wait(inbox.at[pl.ds(0, 2 * reach)], inbox_send)
     for c in range(chunks):
-        part = land.at[c, pl.ds(0, n_ta - 1)]
-        pltpu.make_async_copy(part, part, a2a_send.at[c]).wait()
+        wait(land.at[c, pl.ds(0, n_ta - 1)], a2a_send.at[c])
+    whole.wait()
 
 
 def pick_right(x, onehot):
@@ -277,7 +336,6 @@
 def local(sizes, movie, shifts, footprint, support, neuron_ids, owner_order, start_traces):
     n_ta, n_row = sizes
     _, local_frames, height, breadth = movie.shape
-    patches = shifts.shape[2]
     pixels = TH * TW
     tiles, slots = footprint.shape[1:3]
     neurons = owner_order.shape[0]
@@ -289,6 +347,7 @@
     rows = tiles * CHUNK
     n_dev = n_ta * n_row
     window = -(-(tiles + 2 * REACH) // 8) * 8
+    reach = -(-REACH // tiles)
     band_lanes = -(-(window // 8 * window) // LANES) * LANES
     dma = pltpu.SemaphoreType.DMA
     tile_movie, traces = pl.pallas_call(
@@ -298,31 +357,35 @@
             jax.ShapeDtypeStruct((own, frames), F32),
         ),
         in_specs=[pl.BlockSpec(memory_space=pltpu.SMEM), pl.BlockSpec(memory_space=pl.ANY)] + [vmem] * 7,
-        out_specs=(vmem, vmem),
+        out_specs=(pl.BlockSpec(memory_space=pl.ANY), vmem),
         scratch_shapes=[
             pltpu.VMEM((local_frames, height, breadth), BF16),
             pltpu.VMEM((chunks, n_ta, rows, pixels), BF16),
             pltpu.VMEM((chunks, n_ta, rows, pixels), BF16),
             pltpu.VMEM((pixels // LANES, n_ta * rows, LANES), F32),
             pltpu.VMEM((pixels // LANES, tiles * frames, LANES), F32),
+            pltpu.VMEM((tiles, frames, pixels), BF16),
+            pltpu.VMEM((tiles * slots, pixels), BF16),
             pltpu.VMEM((n_dev, 8, band_lanes), F32),
             pltpu.VMEM((n_dev, own, frames), F32),
-            pltpu.VMEM((n_dev, window, frames), BF16),
+            pltpu.VMEM((2 * reach + 1, tiles, frames), F32),
+            pltpu.VMEM((2 * reach + 1, tiles, frames), F32),
+            pltpu.VMEM((n_dev, tiles, frames), F32),
             pltpu.VMEM((tiles * slots, frames), F32),
-            dma((chunks,)), dma((chunks,)), dma((chunks,)), dma, dma, dma, dma, dma, dma,
+            dma((chunks,)), dma, dma((chunks,)), dma((chunks,)), dma((3, 4)), dma, dma,
         ],
         compiler_params=pltpu.CompilerParams(
             collective_id=0, has_side_effects=True, vmem_limit_bytes=56 * 2**20
         ),
         name="traces",
     )(
-        shifts[0].reshape(local_frames, patches * 2),
+        shifts[0].transpose(1, 2, 0),
         movie[0],
         jnp.asarray(smoothing_table(breadth).astype(jnp.bfloat16)),
         jnp.asarray(tall.astype(jnp.bfloat16)),
         footprint.reshape(tiles * slots, pixels),
         support.reshape(tiles * slots, pixels),
-        neuron_ids.reshape(1, tiles * slots),
+        neuron_ids[0],
         owner_order.reshape(1, neurons),
         start_traces,
     )

time: 53.3 us -> 49.8 us (0.934)
  local copies, waits for them, and re-layouts: 4.78 us -> 2.86 us
  Pallas kernels: 47.6 us -> 45.7 us
    pallas_call x1, Pallas kernels: 47.6 us -> 45.7 us  [local(): pl.pallas_call(functools.partial(trace_kernel, sizes), out_shape=(jax.Sha...]
    unnamed x8 -> x4, local copies, waits for them, and re-layouts: 3.53 us -> 2.86 us
    another operation x1 -> x0, local copies, waits for them, and re-layouts: 0.66 us -> none  [local(): shifts[0].reshape(local_frames, patches * 2)]
    reshape x1 -> x0, local copies, waits for them, and re-layouts: 0.59 us -> none  [local(): neuron_ids.reshape(1, tiles * slots)]
where the time goes in v3:
time: 49.8 us; the launch traced here: 49.2 us
  Pallas kernels  45.7 us (92%)
  local copies, waits for them, and re-layouts  2.86 us (6%)
  between operations  0.65 us (1%)
    pallas_call x1, Pallas kernels, local(): pl.pallas_call(functools.partial(trace_kernel, sizes), out_shape=(jax.Sha...  45.7 us
    unnamed x4, local copies, waits for them, and re-layouts  2.86 us

profile of v3, /device:TPU:0, one launch (start us, length us, event | category | flops | bytes accessed | tf_op | source)
XLA Modules:
  0.0 49.2 jit_solution(14115946164768039716)
XLA Ops:
  0.6 45.7 %traces.1 = (bf16[8,128,512]{2,1,0:T(8,128)(2,1)}, f32[8,128]{1,0:T(8,128)}) custom-call(s32[4,2,8]{2,1,0:T(2,128)} %bitcast.13, bf16[8,128,512]{2,1,0:T(8,128)(2,1)} %bitcast.9, bf16[512,512]{1,0:T(8,128)(2,1)} %constant.4.clone.wide_table, bf16[128,128]{1,0:T(8,128)(2,1)} %constant.5.clone.tall_table, bf16[64,512]{1,0:T(8,128)(2,1)} %bitcast.12, ...), custom_call_target="tpu_custom_call" | custom-call | tf_op jit(solution)/shard_map/traces/pallas_call | solution.py:353
  46.4 0.0 copy-start
  46.4 2.3 %copy.16 = bf16[1,8,128,512]{3,2,1,0:T(8,128)(2,1)} copy(bf16[1,8,128,512]{3,2,1,0:T(8,128)(2,1)} %bitcast.10) | data formatting | bytes 2097152
  48.6 0.0 copy-done
  48.6 0.6 %copy.17 = f32[8,128]{1,0:T(8,128)} copy(f32[8,128]{1,0:T(8,128)S(1)} %copy-done) | data formatting | bytes 8192
Async XLA Ops:
  46.4 2.3 %copy-start = (f32[8,128]{1,0:T(8,128)S(1)}, f32[8,128]{1,0:T(8,128)}, u32[]{:S(2)}) copy-start(f32[8,128]{1,0:T(8,128)} %get-tuple-element.9) | copy-start | bytes 12292

commit v4 on v3

--- a/solution.py
+++ b/solution.py
@@ -103,15 +103,14 @@
     sizes,
     moves, movie, wide_table, tall_table, prints, support, ids, order, start,
     tiles_out, traces_out,
-    frames_in, send, land, stage, full, tiles_vmem, masked_ref, bands, starts, partial, inbox, drives, projected,
-    movie_sem, tiles_sem, a2a_send, a2a_recv, gather_sems, inbox_send, inbox_recv,
+    frames_in, send, land, stage, full, tiles_vmem, masked_ref, bands, starts, drives, projected,
+    movie_sem, tiles_sem, a2a_send, a2a_recv, gather_sems,
 ):
     n_ta, n_row = sizes
     n_dev = n_ta * n_row
     chunks, _, rows, pixels = send.shape
     tiles, frames, _ = tiles_out.shape
-    reach = inbox.shape[0] // 2
-    window = -(-(tiles + 2 * REACH) // 8) * 8
+    window = drives.shape[1]
     folds = window // 8
     neurons = order.shape[1]
     own = start.shape[0]
@@ -132,14 +131,6 @@
             return carry
         lax.fori_loop(1, n_ta, step, 0)
 
-    def near(body):
-        for e in range(2 * reach + 1):
-            if e != reach:
-                body(e, lax.rem(home + e - reach + n_dev, n_dev))
-
-    def device(n):
-        return (lax.rem(n, n_ta), n // n_ta)
-
     def fetch(c):
         piece = pl.ds(c * CHUNK, CHUNK)
         return pltpu.make_async_copy(movie.at[piece], frames_in.at[piece], movie_sem.at[c])
@@ -154,8 +145,7 @@
     along(lambda other: greet((other, row)))
     for k in range(1, n_row):
         greet((ta, lax.rem(row + k, n_row)))
-    near(lambda e, n: greet(device(n)))
-    greeted = n_ta - 1 + n_row - 1 + 2 * reach
+    greeted = n_ta - 1 + n_row - 1
 
     def names(first, count):
         flat = jnp.concatenate([ids[t : t + 1] for t in range(tiles)], axis=1)
@@ -295,25 +285,12 @@
             masked_ref[tile * slots : (tile + 1) * slots], block, (1, 1)
         )
     whole = pltpu.make_async_copy(tiles_vmem, tiles_out, tiles_sem)
-    terms = pick(names((home - reach) * tiles, (2 * reach + 1) * tiles), projected[...])
-    partial[...] = terms.reshape(2 * reach + 1, tiles, frames)
-
-    near(lambda e, n: pltpu.make_async_remote_copy(
-        src_ref=partial.at[e], dst_ref=inbox.at[e],
-        send_sem=inbox_send, recv_sem=inbox_recv,
-        device_id=device(n), device_id_type=MESH,
-    ).start())
+    drives[home] = pick(names(home * tiles - REACH, window), projected[...]).astype(BF16)
+    gather(drives, 2)
     whole.start()
-    wait(inbox.at[pl.ds(0, 2 * reach)], inbox_recv)
-    mine_drive = partial[reach]
-    for e in range(2 * reach + 1):
-        if e != reach:
-            mine_drive = mine_drive + inbox[e]
-    drives[home] = mine_drive
-    gather(drives, 2)
     relay(drives, 2)
     gathered(drives, 2)
-    drive = drives[...].reshape(neurons, frames)
+    drive = mm(places, drives[...].reshape(n_dev * window, frames), (0, 0))
     for iteration in range(ITERS):
         if iteration:
             base = current - mm3(parts, current) * inverse
@@ -322,10 +299,14 @@
 
     for which, buffer in enumerate((bands, starts, drives)):
         sent(buffer, which)
-    wait(inbox.at[pl.ds(0, 2 * reach)], inbox_send)
     for c in range(chunks):
         wait(land.at[c, pl.ds(0, n_ta - 1)], a2a_send.at[c])
     whole.wait()
+
+
+def finish_kernel(tiles_in, traces_in, tiles_out, traces_out):
+    tiles_out[...] = tiles_in[...]
+    traces_out[...] = traces_in[...]
 
 
 def pick_right(x, onehot):
@@ -347,7 +328,6 @@
     rows = tiles * CHUNK
     n_dev = n_ta * n_row
     window = -(-(tiles + 2 * REACH) // 8) * 8
-    reach = -(-REACH // tiles)
     band_lanes = -(-(window // 8 * window) // LANES) * LANES
     dma = pltpu.SemaphoreType.DMA
     tile_movie, traces = pl.pallas_call(
@@ -368,11 +348,9 @@
             pltpu.VMEM((tiles * slots, pixels), BF16),
             pltpu.VMEM((n_dev, 8, band_lanes), F32),
             pltpu.VMEM((n_dev, own, frames), F32),
-            pltpu.VMEM((2 * reach + 1, tiles, frames), F32),
-            pltpu.VMEM((2 * reach + 1, tiles, frames), F32),
-            pltpu.VMEM((n_dev, tiles, frames), F32),
+            pltpu.VMEM((n_dev, window, frames), BF16),
             pltpu.VMEM((tiles * slots, frames), F32),
-            dma((chunks,)), dma, dma((chunks,)), dma((chunks,)), dma((3, 4)), dma, dma,
+            dma((chunks,)), dma, dma((chunks,)), dma((chunks,)), dma((3, 4)),
         ],
         compiler_params=pltpu.CompilerParams(
             collective_id=0, has_side_effects=True, vmem_limit_bytes=56 * 2**20
@@ -389,6 +367,22 @@
         owner_order.reshape(1, neurons),
         start_traces,
     )
+    steps = 2
+    specs = (
+        pl.BlockSpec((tiles, frames // steps, pixels), lambda i: (0, i, 0)),
+        pl.BlockSpec((own, frames), lambda i: (0, 0)),
+    )
+    tile_movie, traces = pl.pallas_call(
+        finish_kernel,
+        grid=(steps,),
+        out_shape=(
+            jax.ShapeDtypeStruct((tiles, frames, pixels), BF16),
+            jax.ShapeDtypeStruct((own, frames), F32),
+        ),
+        in_specs=list(specs),
+        out_specs=specs,
+        name="finish",
+    )(tile_movie, traces)
     return tile_movie[None], traces
 
 

time: 49.8 us -> 45.7 us (0.918)
  local copies, waits for them, and re-layouts: 2.86 us -> 0 us
  Pallas kernels: 45.7 us -> 44.3 us
    pallas_call x1, Pallas kernels: 45.7 us -> 42.2 us  [local(): pl.pallas_call(functools.partial(trace_kernel, sizes), out_shape=(jax.Sha...]
    unnamed x4 -> x0, local copies, waits for them, and re-layouts: 2.86 us -> none
    pallas_call x0 -> x1, Pallas kernels: none -> 2.06 us  [local(): pl.pallas_call(finish_kernel, grid=(steps,), out_shape=(jax.ShapeDtypeStr...]
where the time goes in v4:
time: 45.7 us; the launch traced here: 44.9 us
  Pallas kernels  44.3 us (97%)
  between operations  0.64 us (1%)
    pallas_call x1, Pallas kernels, local(): pl.pallas_call(functools.partial(trace_kernel, sizes), out_shape=(jax.Sha...  42.2 us
    pallas_call x1, Pallas kernels, local(): pl.pallas_call(finish_kernel, grid=(steps,), out_shape=(jax.ShapeDtypeStr...  2.06 us

profile of v4, /device:TPU:0, one launch (start us, length us, event | category | flops | bytes accessed | tf_op | source)
XLA Modules:
  0.0 44.9 jit_solution(18228267457607332704)
XLA Ops:
  0.6 42.2 %traces.1 = (bf16[8,128,512]{2,1,0:T(8,128)(2,1)}, f32[8,128]{1,0:T(8,128)}) custom-call(s32[4,2,8]{2,1,0:T(2,128)} %bitcast.12, bf16[8,128,512]{2,1,0:T(8,128)(2,1)} %bitcast.9, bf16[512,512]{1,0:T(8,128)(2,1)} %constant.4.clone.wide_table, bf16[128,128]{1,0:T(8,128)(2,1)} %constant.5.clone.tall_table, bf16[64,512]{1,0:T(8,128)(2,1)} %bitcast.11, ...), custom_call_target="tpu_custom_call" | custom-call | tf_op jit(solution)/shard_map/traces/pallas_call | solution.py:333
  42.8 2.1 %finish.1 = (bf16[8,128,512]{2,1,0:T(8,128)(2,1)}, f32[8,128]{1,0:T(8,128)}) custom-call(bf16[8,128,512]{2,1,0:T(8,128)(2,1)} %get-tuple-element.6.tiles_in, f32[8,128]{1,0:T(8,128)} %get-tuple-element.7.traces_in), custom_call_target="tpu_custom_call" | custom-call | tf_op jit(solution)/shard_map/finish/pallas_call | solution.py:375

commit v5 on v4

--- a/solution.py
+++ b/solution.py
@@ -236,8 +236,8 @@
     relay(starts, 1)
     gathered(bands, 0)
     gathered(starts, 1)
-    spots = lax.broadcasted_iota(jnp.int32, (n_dev * window, neurons), 0)
-    wanted = lax.broadcasted_iota(jnp.int32, (n_dev * window, neurons), 1)
+    spots = lax.broadcasted_iota(jnp.int32, (neurons, n_dev * window), 1)
+    wanted = lax.broadcasted_iota(jnp.int32, (neurons, n_dev * window), 0)
     named = lax.rem(spots // window * tiles + lax.rem(spots, window) - REACH + neurons, neurons)
     places = (named == wanted).astype(F32).astype(BF16)
     expand_a = lax.broadcasted_iota(jnp.int32, (window, neurons), 0)
@@ -252,7 +252,7 @@
         [(pltpu.roll(wide[n], n * tiles % neurons, 1) if n * tiles % neurons else wide[n])[None] for n in range(n_dev)],
         axis=0,
     ).reshape(n_dev * window, neurons)
-    coupling = pick(places, wide, (0, 0))
+    coupling = pick(places, wide)
     bound = 1.0 + jnp.sum(coupling, axis=1, keepdims=True)
     inverse = 1.0 / bound
     keeper = order[...] // own
@@ -290,7 +290,7 @@
     whole.start()
     relay(drives, 2)
     gathered(drives, 2)
-    drive = mm(places, drives[...].reshape(n_dev * window, frames), (0, 0))
+    drive = mm(places, drives[...].reshape(n_dev * window, frames))
     for iteration in range(ITERS):
         if iteration:
             base = current - mm3(parts, current) * inverse

time: 45.7 us -> 45.7 us (level)
  no operation moved by 1% of the time
where the time goes in v5:
time: 45.7 us; the launch traced here: 44.9 us
  Pallas kernels  44.3 us (97%)
  between operations  0.64 us (1%)
    pallas_call x1, Pallas kernels, local(): pl.pallas_call(functools.partial(trace_kernel, sizes), out_shape=(jax.Sha...  42.2 us
    pallas_call x1, Pallas kernels, local(): pl.pallas_call(finish_kernel, grid=(steps,), out_shape=(jax.ShapeDtypeStr...  2.06 us

profile of v5, /device:TPU:0, one launch (start us, length us, event | category | flops | bytes accessed | tf_op | source)
XLA Modules:
  0.0 44.9 jit_solution(4130078795283167121)
XLA Ops:
  0.6 42.2 %traces.1 = (bf16[8,128,512]{2,1,0:T(8,128)(2,1)}, f32[8,128]{1,0:T(8,128)}) custom-call(s32[4,2,8]{2,1,0:T(2,128)} %bitcast.12, bf16[8,128,512]{2,1,0:T(8,128)(2,1)} %bitcast.9, bf16[512,512]{1,0:T(8,128)(2,1)} %constant.4.clone.wide_table, bf16[128,128]{1,0:T(8,128)(2,1)} %constant.5.clone.tall_table, bf16[64,512]{1,0:T(8,128)(2,1)} %bitcast.11, ...), custom_call_target="tpu_custom_call" | custom-call | tf_op jit(solution)/shard_map/traces/pallas_call | solution.py:333
  42.8 2.1 %finish.1 = (bf16[8,128,512]{2,1,0:T(8,128)(2,1)}, f32[8,128]{1,0:T(8,128)}) custom-call(bf16[8,128,512]{2,1,0:T(8,128)(2,1)} %get-tuple-element.6.tiles_in, f32[8,128]{1,0:T(8,128)} %get-tuple-element.7.traces_in), custom_call_target="tpu_custom_call" | custom-call | tf_op jit(solution)/shard_map/finish/pallas_call | solution.py:375
